TPU v7x, 512 devices: a whole 4x8x8 slice. The times are simulated.
512 devices in a mesh: graph: 16 (over z, core), config: 32 (over y, x).
Axes of the slice: x: 4, y: 8, z: 8, core: 2. Of those that a mesh axis runs over, the one named last changes fastest.
Arguments:
- features: bfloat16 [64, 8192, 128], P('config', 'graph'), may hold values from -6 to 6
- cotangent: bfloat16 [64, 8192, 128], P(None, ('graph', 'config')), may hold values from -6 to 6
- sage_weight: bfloat16 [2, 128, 128], replicated, may hold values from -0.5 to 0.5
- attn_weight: bfloat16 [4, 128, 128], replicated, may hold values from -0.5 to 0.5
- tile_vals: bfloat16 [192, 128, 128], P('graph'), may hold values from -0.375 to 0.375
- tile_dst: int32 [192], P('graph'), may hold values from 0 to 3
- tile_src: int32 [192], P('graph'), may hold values from 0 to 3
- tile_count: int32 [16], P('graph'), may hold values from 3 to 12, as said below
- hub_ids: int32 [128], P('graph'), may hold values from 0 to 8191, as said below
- hub_weight: bfloat16 [8192, 128], P('graph'), may hold values from -0.5 to 0.5
Outputs:
- layer_out: bfloat16 [64, 8192, 128], P(None, ('graph', 'config'))
- grad_features: bfloat16 [64, 8192, 128], P('config', 'graph')
- grad_weights: float32 [16, 6, 128, 128], P('graph')
Inputs may be any that keep to these rules, and one draw needn't show every extreme that they name: Slot t of slab g (t counted within the slab) is live when t < tile_count[g]; some slab has all 12 slots live. `hub_ids`: entries g * 8 to (g+1) * 8 - 1 are distinct nodes of slab g.
All inputs are finite; a program needn't handle non-finite values.
Results may differ from a plain program's by a relative error of at most 0.024.
Values may be sent and summed in bfloat16 or wider, within the bound.
A program may use at most 64 MiB of HBM per device.

v0:
```python
import math
import jax
import jax.numpy as jnp
from jax import lax
from jax.sharding import PartitionSpec as P

HEADS = 4
CAP = 20.0


def attend(queries, key_rows, value_rows):
    layout_count, node_count, feature_width = queries.shape
    head_size = feature_width // HEADS
    split = (layout_count, node_count, HEADS, head_size)
    query_b = queries.reshape(split)
    key_b = key_rows.reshape(split)
    value_b = value_rows.reshape(split)
    scores = jnp.einsum(
        "lkhd,mkhd->khlm", query_b, key_b, preferred_element_type=jnp.float32
    ) / math.sqrt(head_size)
    capped = CAP * jnp.tanh(scores / CAP)
    weights = jnp.exp(capped)
    attention = weights / jnp.sum(weights, axis=-1, keepdims=True)
    attention = attention.astype(value_b.dtype)
    mixture = jnp.einsum("khlm,mkhd->lkhd", attention, value_b, preferred_element_type=jnp.float32)
    return mixture.reshape(layout_count, node_count, feature_width).astype(queries.dtype)


def project(flat_rows, weight):
    return jnp.dot(flat_rows, weight, preferred_element_type=jnp.float32)


def project_back(flat_rows, weight):
    return jnp.dot(flat_rows, weight.T, preferred_element_type=jnp.float32)


def outer_sum(left_rows, right_rows):
    return jnp.dot(left_rows.T, right_rows, preferred_element_type=jnp.float32)


def sage_forward(feats, aggregate, sage_weight):
    shaped = feats.shape
    width_f = shaped[-1]
    pre_acts = project(feats.reshape(-1, width_f), sage_weight[0]) + project(
        aggregate.reshape(-1, width_f), sage_weight[1]
    )
    hidden = jax.nn.silu(pre_acts).astype(jnp.bfloat16)
    return (pre_acts.reshape(shaped), hidden.reshape(shaped))


def node_forward(hidden, attn_weight):
    shaped = hidden.shape
    width_f = shaped[-1]
    three = (shaped[0], -1, width_f)
    flat_hidden = hidden.reshape(-1, width_f)
    queries = project(flat_hidden, attn_weight[0]).astype(jnp.bfloat16)
    key_rows = project(flat_hidden, attn_weight[1]).astype(jnp.bfloat16)
    value_rows = project(flat_hidden, attn_weight[2]).astype(jnp.bfloat16)
    mixture = attend(queries.reshape(three), key_rows.reshape(three), value_rows.reshape(three))
    output = (
        flat_hidden.astype(jnp.float32) + project(mixture.reshape(-1, width_f), attn_weight[3])
    ).astype(jnp.bfloat16)
    return (
        output.reshape(shaped),
        queries.reshape(shaped),
        key_rows.reshape(shaped),
        value_rows.reshape(shaped),
        mixture.reshape(shaped),
    )


def node_backward(cot_rows, hidden, queries, key_rows, value_rows, mixture, attn_weight):
    shaped = hidden.shape
    width_f = shaped[-1]
    three = (shaped[0], -1, width_f)
    flat_cot = cot_rows.reshape(-1, width_f)
    grad_mix = project_back(flat_cot, attn_weight[3]).astype(jnp.bfloat16)
    grad_wo = outer_sum(mixture.reshape(-1, width_f), flat_cot)
    unused, pullback = jax.vjp(attend, queries, key_rows, value_rows)
    grad_q, grad_k, grad_v = pullback(grad_mix.reshape(three))
    flat_q = grad_q.reshape(-1, width_f)
    flat_k = grad_k.reshape(-1, width_f)
    flat_v = grad_v.reshape(-1, width_f)
    grad_hidden = (
        flat_cot.astype(jnp.float32)
        + project_back(flat_q, attn_weight[0])
        + project_back(flat_k, attn_weight[1])
        + project_back(flat_v, attn_weight[2])
    ).astype(jnp.bfloat16)
    flat_hidden = hidden.reshape(-1, width_f)
    grads = jnp.stack(
        [
            outer_sum(flat_hidden, flat_q),
            outer_sum(flat_hidden, flat_k),
            outer_sum(flat_hidden, flat_v),
            grad_wo,
        ]
    )
    return (grad_hidden.reshape(shaped), grads)


def sage_backward(grad_hidden, pre_acts, feats, aggregate, sage_weight):
    shaped = feats.shape
    width_f = shaped[-1]
    flat_pre = pre_acts.reshape(-1, width_f)
    sigmoid_pre = jax.nn.sigmoid(flat_pre)
    grad_pre = (
        grad_hidden.reshape(-1, width_f).astype(jnp.float32)
        * sigmoid_pre
        * (1.0 + flat_pre * (1.0 - sigmoid_pre))
    ).astype(jnp.bfloat16)
    grads = jnp.stack(
        [
            outer_sum(feats.reshape(-1, width_f), grad_pre),
            outer_sum(aggregate.reshape(-1, width_f), grad_pre),
        ]
    )
    grad_self = project_back(grad_pre, sage_weight[0]).astype(jnp.bfloat16).reshape(shaped)
    grad_agg = project_back(grad_pre, sage_weight[1]).astype(jnp.bfloat16).reshape(shaped)
    return (grad_self, grad_agg, grads)


def tile_forward(source, tile_vals, tile_src, tile_dst, live):
    layout_count, node_count, width_f = source.shape
    tile_size = tile_vals.shape[1]
    block_count = node_count // tile_size
    blocks = source.reshape(layout_count, block_count, tile_size, width_f)[:, tile_src]
    products = jnp.einsum("tij,ltjf->tlif", tile_vals, blocks, preferred_element_type=jnp.float32)
    products = products * live[:, None, None, None]
    summed = jax.ops.segment_sum(products, tile_dst, num_segments=block_count)
    return summed.transpose(1, 0, 2, 3).reshape(layout_count, node_count, width_f)


def tile_backward(grad_agg, tile_vals, tile_dst, tile_src, live):
    layout_count, node_count, width_f = grad_agg.shape
    tile_size = tile_vals.shape[1]
    block_count = node_count // tile_size
    blocks = grad_agg.reshape(layout_count, block_count, tile_size, width_f)[:, tile_dst]
    products = jnp.einsum("tij,ltif->tljf", tile_vals, blocks, preferred_element_type=jnp.float32)
    products = products * live[:, None, None, None]
    summed = jax.ops.segment_sum(products, tile_src, num_segments=block_count)
    return summed.transpose(1, 0, 2, 3).reshape(layout_count, node_count, width_f)


def flatten_nodes(arrays):
    return tuple((item.reshape(item.shape[0], -1, item.shape[-1]) for item in arrays))


def local(
    features,
    cotangent,
    sage_weight,
    attn_weight,
    tile_vals,
    tile_dst,
    tile_src,
    tile_count,
    hub_ids,
    hub_weight,
):
    layout_dev, node_dev, width_f = features.shape
    config_count = lax.axis_size("config")
    node_share = node_dev // config_count
    slab_index = lax.axis_index("graph")
    hub_local = hub_ids - slab_index * node_dev
    live = (jnp.arange(tile_dst.shape[0], dtype=jnp.int32) < tile_count[0]).astype(jnp.float32)
    local_hubs = features[:, hub_local]
    columns = hub_weight
    hub_sum = jnp.einsum(
        "nj,ljf->lnf",
        columns,
        lax.all_gather(local_hubs, "graph", axis=1, tiled=True),
        preferred_element_type=jnp.float32,
    )
    aggregate = (tile_forward(features, tile_vals, tile_src, tile_dst, live) + hub_sum).astype(
        jnp.bfloat16
    )
    split_shape = (layout_dev, config_count, node_share, width_f)
    back_shape = (layout_dev * config_count, 1, node_share, width_f)
    received = (
        lax.all_to_all(
            features.reshape(split_shape), "config", split_axis=1, concat_axis=0, tiled=True
        ),
        lax.all_to_all(
            aggregate.reshape(split_shape), "config", split_axis=1, concat_axis=0, tiled=True
        ),
    )
    pre_in, hidden_in = sage_forward(received[0], received[1], sage_weight)
    results = (received[0], received[1], pre_in, hidden_in) + node_forward(hidden_in, attn_weight)
    feats_node, agg_node, pre_node, hidden_node, output, queries, key_rows, value_rows, mixture = (
        flatten_nodes(results)
    )
    grad_hidden, attn_grads = node_backward(
        cotangent, hidden_node, queries, key_rows, value_rows, mixture, attn_weight
    )
    self_node, aggr_node, sage_grads = sage_backward(
        grad_hidden, pre_node, feats_node, agg_node, sage_weight
    )
    self_back, agg_back = (
        lax.all_to_all(
            self_node.reshape(back_shape), "config", split_axis=0, concat_axis=1, tiled=True
        ),
        lax.all_to_all(
            aggr_node.reshape(back_shape), "config", split_axis=0, concat_axis=1, tiled=True
        ),
    )
    grad_self = self_back.reshape(layout_dev, node_dev, width_f)
    grad_agg = agg_back.reshape(layout_dev, node_dev, width_f)
    back_rows = tile_backward(grad_agg, tile_vals, tile_dst, tile_src, live)
    columns = hub_weight
    hub_grads = lax.psum_scatter(
        jnp.einsum("nj,lnf->jlf", columns, grad_agg, preferred_element_type=jnp.float32).astype(
            jnp.bfloat16
        ),
        "graph",
        scatter_dimension=0,
        tiled=True,
    ).astype(jnp.float32)
    totals = grad_self.astype(jnp.float32) + back_rows
    totals = totals.at[:, hub_local].add(jnp.transpose(hub_grads, (1, 0, 2)))
    grad_features = totals.astype(jnp.bfloat16)
    partial_grads = jnp.concatenate([sage_grads, attn_grads], axis=0)
    summed = lax.psum(partial_grads.astype(jnp.bfloat16), "config").astype(jnp.float32)
    scale = 1.0 / math.sqrt(layout_dev * config_count * node_dev)
    return (output, grad_features, (summed * scale)[None])


def solution(mesh):
    return jax.shard_map(
        local,
        mesh=mesh,
        in_specs=(
            P("config", "graph", None),
            P(None, ("graph", "config"), None),
            P(),
            P(),
            P("graph", None, None),
            P("graph"),
            P("graph"),
            P("graph"),
            P("graph"),
            P("graph", None),
        ),
        out_specs=(
            P(None, ("graph", "config"), None),
            P("config", "graph", None),
            P("graph", None, None, None),
        ),
        check_vma=False,
    )
```

profile of v0, /device:TPU:1, one launch (start us, length us, event | category | flops | bytes accessed | tf_op | source)
XLA Modules:
  0.0 400.2 jit_solution(9092489679401032103)
XLA Ops:
  8.0 1.7 copy.116
  9.7 10.5 %all-to-all-start = ((bf16[2,32,16,128]{3,2,0,1:T(8,128)(2,1)}), bf16[2,32,16,128]{3,2,0,1:T(8,128)(2,1)S(1)}, u32[]{:S(2)}, u32[]{:S(2)}) async-start(bf16[2,32,16,128]{3,2,0,1:T(8,128)(2,1)} %copy.116), calls=%async_computation | async-start | bytes 524288 | tf_op jit(solution)/shard_map/all_to_all | solution.py:181
  20.2 0.7 compare_select_fusion
  20.9 0.7 compare_select_fusion.1
  21.6 1.5 gather_fusion.1
  23.8 0.7 compare_select_fusion.2
  24.4 1.6 gather_fusion
  26.1 1.6 multiply_bitcast_fusion.1
  27.7 1.9 copy.118
  29.6 1.8 scatter_fusion
  32.0 24.1 %all-gather = bf16[2,128,128]{2,1,0:T(8,128)(2,1)S(1)} all-gather(bf16[2,8,128]{2,1,0:T(8,128)(2,1)S(1)} %bitcast.206), channel_id=2, replica_groups=mesh['graph'=16,'config'=32] {'graph'}, dimensions={1}, use_global_device_ids=true | all-gather | bytes 69632 | tf_op jit(solution)/shard_map/all_gather | solution.py:172
  56.5 0.7 copy.121
  57.2 9.8 %all-to-all-start.1 = ((bf16[2,32,16,128]{3,2,0,1:T(8,128)(2,1)}), bf16[2,32,16,128]{3,2,0,1:T(8,128)(2,1)S(1)}, u32[]{:S(2)}, u32[]{:S(2)}) async-start(bf16[2,32,16,128]{3,2,0,1:T(8,128)(2,1)} %copy.121), calls=%async_computation.1 | async-start | bytes 524288 | tf_op jit(solution)/shard_map/all_to_all | solution.py:184
  67.3 0.4 reshape.85
  67.7 1.2 copy.127
  68.9 1.3 dynamic-slice
  71.1 7.6 %all-to-all-done.1 = bf16[2,32,16,128]{3,2,0,1:T(8,128)(2,1)S(1)} async-done(((bf16[2,32,16,128]{3,2,0,1:T(8,128)(2,1)}), bf16[2,32,16,128]{3,2,0,1:T(8,128)(2,1)S(1)}, u32[]{:S(2)}, u32[]{:S(2)}) %all-to-all-start.1) | async-done | bytes 262176 | tf_op jit(solution)/shard_map/all_to_all | solution.py:184
  78.7 1.1 multiply_convert_fusion
  80.0 0.9 convolution_convert_fusion.8
  81.1 0.4 reshape_reshape.24
  81.5 1.2 copy.122
  82.7 2.1 reshape_reshape.25
  84.8 1.8 copy.123
  86.6 3.2 fusion.7
  89.8 0.6 copy-done.15
  90.5 0.6 multiply_divide_fusion
  91.5 1.9 copy.124
  93.4 2.8 fusion.6
  96.2 1.0 fusion.4
  97.2 1.5 fusion.9
  98.7 1.2 fusion.8
  99.9 1.5 fusion.10
  101.8 1.6 copy.134
  103.5 0.5 reshape.87
  104.0 2.5 copy.131
  106.5 0.5 reshape.86
  107.0 1.0 convolution_add_fusion.2
  108.1 2.5 copy.137
  110.6 1.2 reshape.88
  111.8 1.3 convolution_add_fusion.1
  113.1 1.5 fusion.18
  114.9 0.9 convolution_convert_fusion.5
  117.0 4.4 %all-to-all-start.3 = ((bf16[64,1,16,128]{3,2,1,0:T(8,128)(2,1)}), bf16[64,1,16,128]{3,2,1,0:T(8,128)(2,1)S(1)}, u32[]{:S(2)}, u32[]{:S(2)}) async-start(bf16[64,1,16,128]{3,2,1,0:T(8,128)(2,1)} %bitcast.37), calls=%async_computation.3 | async-start | bytes 524288 | tf_op jit(solution)/shard_map/all_to_all | solution.py:203
  121.8 0.7 copy-done.12
  122.6 1.6 copy.126
  124.2 0.5 convert_element_type.128
  124.7 1.7 fusion.13
  126.4 0.9 convolution_convert_fusion.6
  127.3 4.5 %all-to-all-done.3 = bf16[64,1,16,128]{3,2,1,0:T(8,128)(2,1)S(1)} async-done(((bf16[64,1,16,128]{3,2,1,0:T(8,128)(2,1)}), bf16[64,1,16,128]{3,2,1,0:T(8,128)(2,1)S(1)}, u32[]{:S(2)}, u32[]{:S(2)}) %all-to-all-start.3) | async-done | bytes 262176 | tf_op jit(solution)/shard_map/all_to_all | solution.py:203
  131.8 5.2 %all-to-all-start.2 = ((bf16[64,1,16,128]{3,2,1,0:T(8,128)(2,1)}), bf16[64,1,16,128]{3,2,1,0:T(8,128)(2,1)S(1)}, u32[]{:S(2)}, u32[]{:S(2)}) async-start(bf16[64,1,16,128]{3,2,1,0:T(8,128)(2,1)} %bitcast.32), calls=%async_computation.2 | async-start | bytes 524288 | tf_op jit(solution)/shard_map/all_to_all | solution.py:200
  137.1 136.0 %all-reduce.4.cloned.1.call-done = bf16[6,128,128]{1,2,0:T(8,128)(2,1)} async-done(((bf16[6,128,128]{1,2,0:T(8,128)(2,1)}), bf16[6,128,128]{1,2,0:T(8,128)(2,1)}) %all-reduce.4.cloned.1.call-update) | async-done | bytes 196624 | tf_op jit(solution)/shard_map/psum | solution.py:223
  273.1 1.0 multiply_bitcast_fusion.2
  274.1 0.9 copy.157
  275.0 0.7 gather_fusion.2
  275.7 1.6 multiply_bitcast_fusion
  277.3 1.9 copy.143
  279.3 1.8 scatter_fusion.1
  281.4 1.2 fusion.19
  282.5 0.8 copy.148
  283.3 0.6 bitcast_add_fusion
  283.9 106.4 %all-reduce.6.cloned.1.call-done = bf16[128,2,128]{2,1,0:T(2,128)(2,1)} async-done(((bf16[128,2,128]{2,1,0:T(2,128)(2,1)}), bf16[128,2,128]{2,1,0:T(2,128)(2,1)}) %all-reduce.6.cloned.1.call-update) | async-done | bytes 65552
  390.3 0.7 dynamic-slice_convert_fusion
  391.0 0.8 scatter_fusion.2
  392.0 0.7 copy.156
  (68 shorter events, 5.1 us)
Async XLA Ops:
  8.0 18.1 %copy-start = (bf16[12,128,128]{2,1,0:T(8,128)(2,1)S(1)}, bf16[12,128,128]{2,1,0:T(8,128)(2,1)}, u32[]{:S(2)}) copy-start(bf16[12,128,128]{2,1,0:T(8,128)(2,1)} %param.14) | copy-start | bytes 1179652
  9.7 47.5 %all-to-all-start = ((bf16[2,32,16,128]{3,2,0,1:T(8,128)(2,1)}), bf16[2,32,16,128]{3,2,0,1:T(8,128)(2,1)S(1)}, u32[]{:S(2)}, u32[]{:S(2)}) async-start(bf16[2,32,16,128]{3,2,0,1:T(8,128)(2,1)} %copy.116), calls=%async_computation | async-start | bytes 524288 | tf_op jit(solution)/shard_map/all_to_all | solution.py:181
  27.7 1.9 copy-start.17
  31.5 24.6 %copy-start.9 = (bf16[512,128]{1,0:T(8,128)(2,1)S(1)}, bf16[512,128]{1,0:T(8,128)(2,1)}, u32[]{:S(2)}) copy-start(bf16[512,128]{1,0:T(8,128)(2,1)} %param.19) | copy-start | bytes 393220
  31.7 35.3 %copy-start.1 = (bf16[64,16,128]{2,1,0:T(8,128)(2,1)S(1)}, bf16[64,16,128]{2,1,0:T(8,128)(2,1)}, u32[]{:S(2)}) copy-start(bf16[64,16,128]{2,1,0:T(8,128)(2,1)} %param.11) | copy-start | bytes 786436
  31.7 35.3 %copy-start.10 = (bf16[4,128,128]{2,1,0:T(8,128)(2,1)S(1)}, bf16[4,128,128]{2,1,0:T(8,128)(2,1)}, u32[]{:S(2)}) copy-start(bf16[4,128,128]{2,1,0:T(8,128)(2,1)} %param.13) | copy-start | bytes 393220
  57.2 13.6 %copy-start.13 = (bf16[2,128,128]{2,1,0:T(8,128)(2,1)S(1)}, bf16[2,128,128]{2,1,0:T(8,128)(2,1)}, u32[]{:S(2)}) copy-start(bf16[2,128,128]{2,1,0:T(8,128)(2,1)} %param.12) | copy-start | bytes 196612
  57.2 21.5 %all-to-all-start.1 = ((bf16[2,32,16,128]{3,2,0,1:T(8,128)(2,1)}), bf16[2,32,16,128]{3,2,0,1:T(8,128)(2,1)S(1)}, u32[]{:S(2)}, u32[]{:S(2)}) async-start(bf16[2,32,16,128]{3,2,0,1:T(8,128)(2,1)} %copy.121), calls=%async_computation.1 | async-start | bytes 524288 | tf_op jit(solution)/shard_map/all_to_all | solution.py:184
  78.7 2.2 copy-start.7
  89.8 0.6 copy-start.15
  93.4 2.9 copy-start.2
  93.4 2.9 copy-start.16
  97.2 1.5 copy-start.3
  98.7 2.7 copy-start.4
  99.9 1.9 copy-start.5
  103.4 3.6 copy-start.11
  113.1 1.8 copy-start.14
  113.1 2.8 copy-start.8
  114.6 2.1 copy-start.6
  117.0 14.8 %all-to-all-start.3 = ((bf16[64,1,16,128]{3,2,1,0:T(8,128)(2,1)}), bf16[64,1,16,128]{3,2,1,0:T(8,128)(2,1)S(1)}, u32[]{:S(2)}, u32[]{:S(2)}) async-start(bf16[64,1,16,128]{3,2,1,0:T(8,128)(2,1)} %bitcast.37), calls=%async_computation.3 | async-start | bytes 524288 | tf_op jit(solution)/shard_map/all_to_all | solution.py:203
  121.4 151.7 %all-reduce.4.cloned.1.call-start = ((), (), s32[]{:S(2)}) async-start(), calls=%async_computation.4 | async-start | bytes 393216 | tf_op jit(solution)/shard_map/psum | solution.py:223
  121.8 0.7 copy-start.12
  131.8 149.3 %all-to-all-start.2 = ((bf16[64,1,16,128]{3,2,1,0:T(8,128)(2,1)}), bf16[64,1,16,128]{3,2,1,0:T(8,128)(2,1)S(1)}, u32[]{:S(2)}, u32[]{:S(2)}) async-start(bf16[64,1,16,128]{3,2,1,0:T(8,128)(2,1)} %bitcast.32), calls=%async_computation.2 | async-start | bytes 524288 | tf_op jit(solution)/shard_map/all_to_all | solution.py:200
  137.0 253.3 %all-reduce.6.cloned.1.call-start = ((), (), s32[]{:S(2)}) async-start(), calls=%async_computation.5 | async-start | bytes 131072
  277.3 1.9 copy-start.18
Sparse Core Ops, SparseCore 0:
  126.0 147.0 all-reduce.3
Sparse Core Ops, SparseCore 1:
  283.4 106.9 all-reduce.5
where the time goes:
time: 401 us; the launch traced here: 400 us
  waiting for transfers between devices  255 us (64%)
  local copies, waits for them, and re-layouts  36.5 us (9%)
  starting transfers between devices  30 us (7%)
  matrix products  27.2 us (7%)
  blocking collectives  24.1 us (6%)
  between operations  17.4 us (4%)
  other arithmetic  10.5 us (3%)
    psum x1, waiting for transfers between devices, local(): lax.psum(partial_grads.astype(jnp.bfloat16), 'config').astype(jnp.float32)  136 us
    unnamed x3, waiting for transfers between devices  106 us
    all_gather x1, blocking collectives, local(): lax.all_gather(local_hubs, 'graph', axis=1, tiled=True)  24.1 us
    all_to_all x1, starting transfers between devices, local(): lax.all_to_all(features.reshape(split_shape), 'config', split_axis=1, con...  10.5 us
    all_to_all x1, starting transfers between devices, local(): lax.all_to_all(aggregate.reshape(split_shape), 'config', split_axis=1, co...  9.81 us
  transfers between devices with their start and end apart: 6, of which 4 were waited for; matrix products, arithmetic and copies ran while one was open for 7% of the time, Pallas kernels for 0%

commit v1 on v0

--- a/solution.py
+++ b/solution.py
@@ -166,11 +166,35 @@
     live = (jnp.arange(tile_dst.shape[0], dtype=jnp.int32) < tile_count[0]).astype(jnp.float32)
     local_hubs = features[:, hub_local]
     columns = hub_weight
-    hub_sum = jnp.einsum(
-        "nj,ljf->lnf",
-        columns,
-        lax.all_gather(local_hubs, "graph", axis=1, tiled=True),
-        preferred_element_type=jnp.float32,
+
+    def report_cells_here(own_rows, dim_k, inputs):
+        r2 = lax.axis_size("graph")
+        last, out_arr, block_out = (r2, lax.axis_index("graph"), own_rows.shape[dim_k])
+        found = [(p, (p + 1) % last) for p in range(last)]
+        parts_out = last // 2
+        all_rows = p_next = own_rows
+        row_list = [(p, (p - 1) % last) for p in range(last)]
+        b = 1
+        y2 = inputs(own_rows, out_arr * block_out)
+        while b < parts_out + 1:
+            all_rows = lax.ppermute(all_rows, "graph", perm=found)
+            if b < last - parts_out:
+                p_next = lax.ppermute(p_next, "graph", perm=row_list)
+                y2 = y2 + inputs(p_next, (out_arr + b) % last * block_out)
+            w1 = inputs(all_rows, (out_arr - b) % last * block_out)
+            y2 = y2 + w1
+            b += 1
+        return y2
+
+    hub_sum = report_cells_here(
+        local_hubs,
+        1,
+        lambda shard, offset: jnp.einsum(
+            "nj,ljf->lnf",
+            lax.dynamic_slice_in_dim(columns, offset, shard.shape[1], axis=1),
+            shard,
+            preferred_element_type=jnp.float32,
+        ),
     )
     aggregate = (tile_forward(features, tile_vals, tile_src, tile_dst, live) + hub_sum).astype(
         jnp.bfloat16

time: 401 us -> 414 us (1.032)
  starting transfers between devices: 30 us -> 55.8 us
  blocking collectives: 24.1 us -> 0 us
  waiting for transfers between devices: 255 us -> 261 us
  matrix products: 27.2 us -> 32.7 us
    ppermute x0 -> x15, starting transfers between devices: none -> 31 us  [the longest x7 30.2 us: report_cells_here(): p_next = lax.ppermute(p_next, 'graph', perm=row_list)]
    all_gather x1 -> x0, blocking collectives: 24.1 us -> none  [local(): lax.all_gather(local_hubs, 'graph', axis=1, tiled=True)]
    dot_general x1 -> x16, matrix products: 0.24 us -> 6.77 us  [local(): jnp.einsum('nj,ljf->lnf', lax.dynamic_slice_in_dim(columns, offset, shard...]
  transfers between devices with their start and end apart: 6 -> 21, of which waited for: 4 -> 10; matrix products, arithmetic and copies ran while one was open for 7% -> 8% of each run, Pallas kernels for 0% -> 0%
where the time goes in v1:
time: 414 us; the launch traced here: 413 us
  waiting for transfers between devices  261 us (63%)
  starting transfers between devices  55.8 us (13%)
  local copies, waits for them, and re-layouts  35 us (8%)
  matrix products  32.7 us (8%)
  between operations  18 us (4%)
  other arithmetic  10.6 us (3%)
    psum x1, waiting for transfers between devices, local(): lax.psum(partial_grads.astype(jnp.bfloat16), 'config').astype(jnp.float32)  139 us
    unnamed x3, waiting for transfers between devices  106 us
    ppermute x7, starting transfers between devices, report_cells_here(): p_next = lax.ppermute(p_next, 'graph', perm=row_list)  30.2 us
    all_to_all x1, starting transfers between devices, local(): lax.all_to_all(aggregate.reshape(split_shape), 'config', split_axis=1, co...  9.73 us
  transfers between devices with their start and end apart: 21, of which 10 were waited for; matrix products, arithmetic and copies ran while one was open for 8% of the time, Pallas kernels for 0%

profile of v1, /device:TPU:1, one launch (start us, length us, event | category | flops | bytes accessed | tf_op | source)
XLA Modules:
  0.0 412.7 jit_solution(3421154221284668698)
XLA Ops:
  8.0 0.7 compare_select_fusion
  9.4 1.5 gather_fusion.1
  11.0 6.9 %collective-permute-start = (bf16[2,8,128]{2,1,0:T(8,128)(2,1)S(1)}, bf16[2,8,128]{2,1,0:T(8,128)(2,1)S(1)}, u32[]{:S(2)}, u32[]{:S(2)}) collective-permute-start(bf16[2,8,128]{2,1,0:T(8,128)(2,1)S(1)} %bitcast.281), channel_id=1, source_target_pairs={{0,480},{32,0},{64,32},{96,64},{128,96},{160,128},{192,160},{224,1... | collective-permute-start | bytes 12296 | tf_op jit(solution)/shard_map/ppermute | solution.py:182
  17.8 1.7 copy.164
  19.5 6.4 %all-to-all-start = ((bf16[2,32,16,128]{3,2,0,1:T(8,128)(2,1)}), bf16[2,32,16,128]{3,2,0,1:T(8,128)(2,1)}, u32[]{:S(2)}, u32[]{:S(2)}) async-start(bf16[2,32,16,128]{3,2,0,1:T(8,128)(2,1)} %copy.164), calls=%async_computation | async-start | bytes 524288 | tf_op jit(solution)/shard_map/all_to_all | solution.py:205
  26.8 0.7 compare_select_fusion.2
  27.5 2.0 fusion.66
  29.5 0.7 gather_fusion
  31.2 1.9 scatter_fusion
  33.8 0.8 collective-permute-start.3
  34.5 6.0 %collective-permute-start.2 = (bf16[2,8,128]{2,1,0:T(8,128)(2,1)S(1)}, bf16[2,8,128]{2,1,0:T(8,128)(2,1)S(1)}, u32[]{:S(2)}, u32[]{:S(2)}) collective-permute-start(bf16[2,8,128]{2,1,0:T(8,128)(2,1)S(1)} %collective-permute-done), channel_id=1, source_target_pairs={{0,480},{32,0},{64,32},{96,64},{128,96},{160,128},{192,160},{224,1... | collective-permute-start | bytes 12296 | tf_op jit(solution)/shard_map/ppermute | solution.py:182
  41.6 3.5 collective-permute-start.4
  45.9 3.5 collective-permute-start.6
  50.2 3.4 collective-permute-start.8
  54.5 3.4 collective-permute-start.10
  58.7 3.4 collective-permute-start.12
  63.3 3.4 collective-permute-done.14
  67.2 0.7 copy.185
  67.9 9.7 %all-to-all-start.1 = ((bf16[2,32,16,128]{3,2,0,1:T(8,128)(2,1)}), bf16[2,32,16,128]{3,2,0,1:T(8,128)(2,1)S(1)}, u32[]{:S(2)}, u32[]{:S(2)}) async-start(bf16[2,32,16,128]{3,2,0,1:T(8,128)(2,1)} %copy.185), calls=%async_computation.1 | async-start | bytes 524288 | tf_op jit(solution)/shard_map/all_to_all | solution.py:208
  78.3 1.2 copy.191
  79.5 1.3 dynamic-slice
  81.4 1.2 fusion.96
  82.6 5.3 %all-to-all-done.1 = bf16[2,32,16,128]{3,2,0,1:T(8,128)(2,1)S(1)} async-done(((bf16[2,32,16,128]{3,2,0,1:T(8,128)(2,1)}), bf16[2,32,16,128]{3,2,0,1:T(8,128)(2,1)S(1)}, u32[]{:S(2)}, u32[]{:S(2)}) %all-to-all-start.1) | async-done | bytes 262176 | tf_op jit(solution)/shard_map/all_to_all | solution.py:208
  87.9 1.0 multiply_convert_fusion
  89.2 0.9 convolution_convert_fusion.8
  90.7 1.2 copy.186
  91.9 2.1 reshape_reshape.25
  94.0 1.8 copy.187
  95.8 3.2 fusion.7
  100.7 1.8 copy.188
  102.6 2.8 fusion.6
  105.4 1.0 fusion.4
  106.5 1.5 fusion.9
  107.9 1.2 fusion.8
  109.1 1.5 fusion.10
  111.0 1.6 copy.198
  113.1 2.5 copy.195
  116.2 1.0 convolution_add_fusion.2
  117.2 2.5 copy.201
  119.7 1.2 reshape.88
  121.0 1.3 convolution_add_fusion.1
  122.3 1.5 fusion.25
  123.8 1.3 fusion.31
  125.1 0.9 convolution_convert_fusion.5
  127.2 3.9 all-to-all-start.3
  131.5 0.7 copy-done.13
  132.2 1.6 copy.190
  134.3 0.9 fusion.20
  135.3 0.9 convolution_convert_fusion.6
  136.2 5.4 %all-to-all-done.3 = bf16[64,1,16,128]{3,2,1,0:T(8,128)(2,1)S(1)} async-done(((bf16[64,1,16,128]{3,2,1,0:T(8,128)(2,1)}), bf16[64,1,16,128]{3,2,1,0:T(8,128)(2,1)S(1)}, u32[]{:S(2)}, u32[]{:S(2)}) %all-to-all-start.3) | async-done | bytes 262176 | tf_op jit(solution)/shard_map/all_to_all | solution.py:227
  141.6 4.6 %all-to-all-start.2 = ((bf16[64,1,16,128]{3,2,1,0:T(8,128)(2,1)}), bf16[64,1,16,128]{3,2,1,0:T(8,128)(2,1)}, u32[]{:S(2)}, u32[]{:S(2)}) async-start(bf16[64,1,16,128]{3,2,1,0:T(8,128)(2,1)} %bitcast.47), calls=%async_computation.2 | async-start | bytes 524288 | tf_op jit(solution)/shard_map/all_to_all | solution.py:224
  146.3 139.3 %all-reduce.4.cloned.1.call-done = bf16[6,128,128]{1,2,0:T(8,128)(2,1)} async-done(((bf16[6,128,128]{1,2,0:T(8,128)(2,1)}), bf16[6,128,128]{1,2,0:T(8,128)(2,1)}) %all-reduce.4.cloned.1.call-update) | async-done | bytes 196624 | tf_op jit(solution)/shard_map/psum | solution.py:247
  285.6 1.0 multiply_bitcast_fusion.2
  286.6 0.9 copy.221
  287.5 0.7 gather_fusion.2
  288.2 1.6 multiply_bitcast_fusion
  289.8 1.9 copy.207
  291.8 1.8 scatter_fusion.1
  293.7 1.2 copy.203
  295.1 0.8 copy.212
  296.5 106.4 %all-reduce.6.cloned.1.call-done = bf16[128,2,128]{2,1,0:T(2,128)(2,1)} async-done(((bf16[128,2,128]{2,1,0:T(2,128)(2,1)}), bf16[128,2,128]{2,1,0:T(2,128)(2,1)}) %all-reduce.6.cloned.1.call-update) | async-done | bytes 65552
  402.9 0.7 dynamic-slice_convert_fusion
  403.6 0.8 scatter_fusion.2
  404.5 0.7 copy.220
  (120 shorter events, 15.6 us)
Async XLA Ops:
  8.0 22.2 %copy-start = (bf16[12,128,128]{2,1,0:T(8,128)(2,1)S(1)}, bf16[12,128,128]{2,1,0:T(8,128)(2,1)}, u32[]{:S(2)}) copy-start(bf16[12,128,128]{2,1,0:T(8,128)(2,1)} %param.14) | copy-start | bytes 1179652
  8.0 21.5 %copy-start.2 = (bf16[2,512,128]{2,1,0:T(8,128)(2,1)S(1)}, bf16[2,512,128]{2,1,0:T(8,128)(2,1)}, u32[]{:S(2)}) copy-start(bf16[2,512,128]{2,1,0:T(8,128)(2,1)} %param.10) | copy-start | bytes 786436
  9.4 20.1 %copy-start.20 = (s32[8]{0:T(128)}, s32[8]{0:T(128)S(1)}, u32[]{:S(2)}) copy-start(s32[8]{0:T(128)S(1)} %compare_select_fusion.1) | copy-start | bytes 100
  11.0 23.6 %collective-permute-start = (bf16[2,8,128]{2,1,0:T(8,128)(2,1)S(1)}, bf16[2,8,128]{2,1,0:T(8,128)(2,1)S(1)}, u32[]{:S(2)}, u32[]{:S(2)}) collective-permute-start(bf16[2,8,128]{2,1,0:T(8,128)(2,1)S(1)} %bitcast.281), channel_id=1, source_target_pairs={{0,480},{32,0},{64,32},{96,64},{128,96},{160,128},{192,160},{224,1... | collective-permute-start | bytes 12296 | tf_op jit(solution)/shard_map/ppermute | solution.py:182
  17.8 15.9 %collective-permute-start.1 = (bf16[2,8,128]{2,1,0:T(8,128)(2,1)S(1)}, bf16[2,8,128]{2,1,0:T(8,128)(2,1)S(1)}, u32[]{:S(2)}, u32[]{:S(2)}) collective-permute-start(bf16[2,8,128]{2,1,0:T(8,128)(2,1)S(1)} %bitcast.282), channel_id=1, source_target_pairs={{0,32},{32,64},{64,96},{96,128},{128,160},{160,192},{192,224},{224... | collective-permute-start | bytes 12296 | tf_op jit(solution)/shard_map/ppermute | solution.py:180
  19.5 48.4 %all-to-all-start = ((bf16[2,32,16,128]{3,2,0,1:T(8,128)(2,1)}), bf16[2,32,16,128]{3,2,0,1:T(8,128)(2,1)}, u32[]{:S(2)}, u32[]{:S(2)}) async-start(bf16[2,32,16,128]{3,2,0,1:T(8,128)(2,1)} %copy.164), calls=%async_computation | async-start | bytes 524288 | tf_op jit(solution)/shard_map/all_to_all | solution.py:205
  26.8 3.8 copy-start.18
  33.2 7.4 %copy-start.1 = (bf16[512,128]{1,0:T(8,128)(2,1)S(1)}, bf16[512,128]{1,0:T(8,128)(2,1)}, u32[]{:S(2)}) copy-start(bf16[512,128]{1,0:T(8,128)(2,1)} %param.19) | copy-start | bytes 393220
  33.2 7.4 %copy-start.5 = (f32[2,128,512]{2,1,0:T(8,128)S(1)}, f32[2,128,512]{2,1,0:T(8,128)}, u32[]{:S(2)}) copy-start(f32[2,128,512]{2,1,0:T(8,128)} %fusion.66) | copy-start | bytes 1572868
  33.8 7.5 %collective-permute-start.3 = (bf16[2,8,128]{2,1,0:T(8,128)(2,1)S(1)}, bf16[2,8,128]{2,1,0:T(8,128)(2,1)S(1)}, u32[]{:S(2)}, u32[]{:S(2)}) collective-permute-start(bf16[2,8,128]{2,1,0:T(8,128)(2,1)S(1)} %collective-permute-done.1), channel_id=1, source_target_pairs={{0,32},{32,64},{64,96},{96,128},{128,160},{160,192},{192,224},{224... | collective-permute-start | bytes 12296 | tf_op jit(solution)/shard_map/ppermute | solution.py:180
  34.5 7.0 %collective-permute-start.2 = (bf16[2,8,128]{2,1,0:T(8,128)(2,1)S(1)}, bf16[2,8,128]{2,1,0:T(8,128)(2,1)S(1)}, u32[]{:S(2)}, u32[]{:S(2)}) collective-permute-start(bf16[2,8,128]{2,1,0:T(8,128)(2,1)S(1)} %collective-permute-done), channel_id=1, source_target_pairs={{0,480},{32,0},{64,32},{96,64},{128,96},{160,128},{192,160},{224,1... | collective-permute-start | bytes 12296 | tf_op jit(solution)/shard_map/ppermute | solution.py:182
  41.2 4.2 %collective-permute-start.5 = (bf16[2,8,128]{2,1,0:T(8,128)(2,1)S(1)}, bf16[2,8,128]{2,1,0:T(8,128)(2,1)S(1)}, u32[]{:S(2)}, u32[]{:S(2)}) collective-permute-start(bf16[2,8,128]{2,1,0:T(8,128)(2,1)S(1)} %collective-permute-done.3), channel_id=1, source_target_pairs={{0,32},{32,64},{64,96},{96,128},{128,160},{160,192},{192,224},{224... | collective-permute-start | bytes 12296 | tf_op jit(solution)/shard_map/ppermute | solution.py:180
  41.6 4.3 %collective-permute-start.4 = (bf16[2,8,128]{2,1,0:T(8,128)(2,1)S(1)}, bf16[2,8,128]{2,1,0:T(8,128)(2,1)S(1)}, u32[]{:S(2)}, u32[]{:S(2)}) collective-permute-start(bf16[2,8,128]{2,1,0:T(8,128)(2,1)S(1)} %collective-permute-done.2), channel_id=1, source_target_pairs={{0,480},{32,0},{64,32},{96,64},{128,96},{160,128},{192,160},{224,1... | collective-permute-start | bytes 12296 | tf_op jit(solution)/shard_map/ppermute | solution.py:182
  45.5 4.3 %collective-permute-start.7 = (bf16[2,8,128]{2,1,0:T(8,128)(2,1)S(1)}, bf16[2,8,128]{2,1,0:T(8,128)(2,1)S(1)}, u32[]{:S(2)}, u32[]{:S(2)}) collective-permute-start(bf16[2,8,128]{2,1,0:T(8,128)(2,1)S(1)} %collective-permute-done.5), channel_id=1, source_target_pairs={{0,32},{32,64},{64,96},{96,128},{128,160},{160,192},{192,224},{224... | collective-permute-start | bytes 12296 | tf_op jit(solution)/shard_map/ppermute | solution.py:180
  45.9 4.3 %collective-permute-start.6 = (bf16[2,8,128]{2,1,0:T(8,128)(2,1)S(1)}, bf16[2,8,128]{2,1,0:T(8,128)(2,1)S(1)}, u32[]{:S(2)}, u32[]{:S(2)}) collective-permute-start(bf16[2,8,128]{2,1,0:T(8,128)(2,1)S(1)} %collective-permute-done.4), channel_id=1, source_target_pairs={{0,480},{32,0},{64,32},{96,64},{128,96},{160,128},{192,160},{224,1... | collective-permute-start | bytes 12296 | tf_op jit(solution)/shard_map/ppermute | solution.py:182
  49.7 4.2 %collective-permute-start.9 = (bf16[2,8,128]{2,1,0:T(8,128)(2,1)S(1)}, bf16[2,8,128]{2,1,0:T(8,128)(2,1)S(1)}, u32[]{:S(2)}, u32[]{:S(2)}) collective-permute-start(bf16[2,8,128]{2,1,0:T(8,128)(2,1)S(1)} %collective-permute-done.7), channel_id=1, source_target_pairs={{0,32},{32,64},{64,96},{96,128},{128,160},{160,192},{192,224},{224... | collective-permute-start | bytes 12296 | tf_op jit(solution)/shard_map/ppermute | solution.py:180
  50.2 4.2 %collective-permute-start.8 = (bf16[2,8,128]{2,1,0:T(8,128)(2,1)S(1)}, bf16[2,8,128]{2,1,0:T(8,128)(2,1)S(1)}, u32[]{:S(2)}, u32[]{:S(2)}) collective-permute-start(bf16[2,8,128]{2,1,0:T(8,128)(2,1)S(1)} %collective-permute-done.6), channel_id=1, source_target_pairs={{0,480},{32,0},{64,32},{96,64},{128,96},{160,128},{192,160},{224,1... | collective-permute-start | bytes 12296 | tf_op jit(solution)/shard_map/ppermute | solution.py:182
  54.0 4.2 %collective-permute-start.11 = (bf16[2,8,128]{2,1,0:T(8,128)(2,1)S(1)}, bf16[2,8,128]{2,1,0:T(8,128)(2,1)S(1)}, u32[]{:S(2)}, u32[]{:S(2)}) collective-permute-start(bf16[2,8,128]{2,1,0:T(8,128)(2,1)S(1)} %collective-permute-done.9), channel_id=1, source_target_pairs={{0,32},{32,64},{64,96},{96,128},{128,160},{160,192},{192,224},{224... | collective-permute-start | bytes 12296 | tf_op jit(solution)/shard_map/ppermute | solution.py:180
  54.5 4.2 %collective-permute-start.10 = (bf16[2,8,128]{2,1,0:T(8,128)(2,1)S(1)}, bf16[2,8,128]{2,1,0:T(8,128)(2,1)S(1)}, u32[]{:S(2)}, u32[]{:S(2)}) collective-permute-start(bf16[2,8,128]{2,1,0:T(8,128)(2,1)S(1)} %collective-permute-done.8), channel_id=1, source_target_pairs={{0,480},{32,0},{64,32},{96,64},{128,96},{160,128},{192,160},{224,1... | collective-permute-start | bytes 12296 | tf_op jit(solution)/shard_map/ppermute | solution.py:182
  58.2 4.2 %collective-permute-start.13 = (bf16[2,8,128]{2,1,0:T(8,128)(2,1)S(1)}, bf16[2,8,128]{2,1,0:T(8,128)(2,1)S(1)}, u32[]{:S(2)}, u32[]{:S(2)}) collective-permute-start(bf16[2,8,128]{2,1,0:T(8,128)(2,1)S(1)} %collective-permute-done.11), channel_id=1, source_target_pairs={{0,32},{32,64},{64,96},{96,128},{128,160},{160,192},{192,224},{224... | collective-permute-start | bytes 12296 | tf_op jit(solution)/shard_map/ppermute | solution.py:180
  58.7 4.2 %collective-permute-start.12 = (bf16[2,8,128]{2,1,0:T(8,128)(2,1)S(1)}, bf16[2,8,128]{2,1,0:T(8,128)(2,1)S(1)}, u32[]{:S(2)}, u32[]{:S(2)}) collective-permute-start(bf16[2,8,128]{2,1,0:T(8,128)(2,1)S(1)} %collective-permute-done.10), channel_id=1, source_target_pairs={{0,480},{32,0},{64,32},{96,64},{128,96},{160,128},{192,160},{224,1... | collective-permute-start | bytes 12296 | tf_op jit(solution)/shard_map/ppermute | solution.py:182
  62.5 4.2 %collective-permute-start.14 = (bf16[2,8,128]{2,1,0:T(8,128)(2,1)S(1)}, bf16[2,8,128]{2,1,0:T(8,128)(2,1)S(1)}, u32[]{:S(2)}, u32[]{:S(2)}) collective-permute-start(bf16[2,8,128]{2,1,0:T(8,128)(2,1)S(1)} %collective-permute-done.13), channel_id=1, source_target_pairs={{0,32},{32,64},{64,96},{96,128},{128,160},{160,192},{192,224},{224... | collective-permute-start | bytes 12296 | tf_op jit(solution)/shard_map/ppermute | solution.py:180
  62.8 14.8 %copy-start.3 = (bf16[64,16,128]{2,1,0:T(8,128)(2,1)S(1)}, bf16[64,16,128]{2,1,0:T(8,128)(2,1)}, u32[]{:S(2)}) copy-start(bf16[64,16,128]{2,1,0:T(8,128)(2,1)} %param.11) | copy-start | bytes 786436
  62.8 14.8 %copy-start.12 = (bf16[4,128,128]{2,1,0:T(8,128)(2,1)S(1)}, bf16[4,128,128]{2,1,0:T(8,128)(2,1)}, u32[]{:S(2)}) copy-start(bf16[4,128,128]{2,1,0:T(8,128)(2,1)} %param.13) | copy-start | bytes 393220
  67.9 13.5 %copy-start.14 = (bf16[2,128,128]{2,1,0:T(8,128)(2,1)S(1)}, bf16[2,128,128]{2,1,0:T(8,128)(2,1)}, u32[]{:S(2)}) copy-start(bf16[2,128,128]{2,1,0:T(8,128)(2,1)} %param.12) | copy-start | bytes 196612
  67.9 20.0 %all-to-all-start.1 = ((bf16[2,32,16,128]{3,2,0,1:T(8,128)(2,1)}), bf16[2,32,16,128]{3,2,0,1:T(8,128)(2,1)S(1)}, u32[]{:S(2)}, u32[]{:S(2)}) async-start(bf16[2,32,16,128]{3,2,0,1:T(8,128)(2,1)} %copy.185), calls=%async_computation.1 | async-start | bytes 524288 | tf_op jit(solution)/shard_map/all_to_all | solution.py:208
  87.9 2.2 copy-start.10
  99.1 0.6 copy-start.16
  102.6 2.9 copy-start.4
  102.6 2.9 copy-start.17
  106.4 1.5 copy-start.6
  107.9 2.7 copy-start.7
  109.1 1.9 copy-start.8
  122.2 2.8 copy-start.15
  122.2 3.7 copy-start.11
  123.8 3.1 copy-start.9
  127.2 14.5 %all-to-all-start.3 = ((bf16[64,1,16,128]{3,2,1,0:T(8,128)(2,1)}), bf16[64,1,16,128]{3,2,1,0:T(8,128)(2,1)S(1)}, u32[]{:S(2)}, u32[]{:S(2)}) async-start(bf16[64,1,16,128]{3,2,1,0:T(8,128)(2,1)} %bitcast.52), calls=%async_computation.3 | async-start | bytes 524288 | tf_op jit(solution)/shard_map/all_to_all | solution.py:227
  131.1 154.5 %all-reduce.4.cloned.1.call-start = ((), (), s32[]{:S(2)}) async-start(), calls=%async_computation.4 | async-start | bytes 393216 | tf_op jit(solution)/shard_map/psum | solution.py:247
  131.5 0.7 copy-start.13
  136.2 152.0 %copy-start.19 = (f32[12]{0:T(128)S(1)}, f32[12]{0:T(128)}, u32[]{:S(2)}) copy-start(f32[12]{0:T(128)} %copy-done.18) | copy-start | bytes 148
  141.6 152.0 %all-to-all-start.2 = ((bf16[64,1,16,128]{3,2,1,0:T(8,128)(2,1)}), bf16[64,1,16,128]{3,2,1,0:T(8,128)(2,1)}, u32[]{:S(2)}, u32[]{:S(2)}) async-start(bf16[64,1,16,128]{3,2,1,0:T(8,128)(2,1)} %bitcast.47), calls=%async_computation.2 | async-start | bytes 524288 | tf_op jit(solution)/shard_map/all_to_all | solution.py:224
  146.2 256.6 %all-reduce.6.cloned.1.call-start = ((), (), s32[]{:S(2)}) async-start(), calls=%async_computation.5 | async-start | bytes 131072
  289.8 1.9 copy-start.22
  293.6 110.0 %copy-start.21 = (s32[8]{0:T(128)S(1)}, s32[8]{0:T(128)}, u32[]{:S(2)}) copy-start(s32[8]{0:T(128)} %copy-done.20) | copy-start | bytes 100
Sparse Core Ops, SparseCore 0:
  135.7 149.8 all-reduce.3
Sparse Core Ops, SparseCore 1:
  296.0 106.9 all-reduce.5
